TPU v7x, 256 devices: a whole 4x4x8 slice. The times are simulated.
256 devices in a mesh: vir: 16 (over x, z_lo, core), occ: 16 (over z_hi, y).
Axes of the slice: x: 4, y: 4, z: 8 (z_hi: 4, z_lo: 2; z = z_hi * 2 + z_lo), core: 2. Of those that a mesh axis runs over, the one named last changes fastest.
Arguments:
- amplitudes: bfloat16 [16384, 8192], P('occ'), may hold values from -6 to 6
- integrals: bfloat16 [8192, 8192], P('occ', 'vir'), may hold values from -0.1875 to 0.1875
- tile_irrep: int32 [64], replicated, may hold values from 0 to 3
- tile_spin: int32 [64], replicated, may hold values from 0 to 1
- row_mirror: int32 [16384], P('occ'), may hold values from 0 to 16383, as said below
- col_mirror: int32 [8192], P('vir'), may hold values from 0 to 8191, as said below
- occ_gap: float32 [16384], P('occ'), may hold values from 0.5 to 2
- vir_energy: float32 [8192], P('vir'), may hold values from 0.5 to 4
Outputs:
- new_amps: float32 [16384, 8192], P('occ', 'vir')
Inputs may be any that keep to these rules, and one draw needn't show every extreme that they name: row_mirror is an involution with no fixed point; a row of occupied block k (blocks of 1024 rows in order) has its mirror in block (k + 8) modulo 16. col_mirror is an involution with no fixed point; a pair of virtual block k (blocks of 512 pairs in order) has its mirror in block (k + 8) modulo 16.
All inputs are finite; a program needn't handle non-finite values.
Results may differ from a plain program's by a relative error of at most 0.0003.
Values may be sent and summed in bfloat16 or wider, within the bound.
A program may use at most 128 MiB of HBM per device.

v0:
```python
import jax
import jax.numpy as jnp
from jax import lax
from jax.sharding import PartitionSpec as P

TILE = 128
SPINS = 2


def from_partner(x, axis, apart):
    return lax.ppermute(x, axis, [(i, i ^ 1 << apart) for i in range(lax.axis_size(axis))])


def local(
    amplitudes, integrals, tile_irrep, tile_spin, row_mirror, col_mirror, occ_gap, vir_energy
):
    row_count, col_count = integrals.shape
    row_tiles = row_count // TILE
    col_tiles = col_count // TILE
    code = tile_irrep * SPINS + tile_spin
    row_codes = lax.dynamic_slice_in_dim(code, lax.axis_index("occ") * row_tiles, row_tiles)
    col_codes = lax.dynamic_slice_in_dim(code, lax.axis_index("vir") * col_tiles, col_tiles)
    allowed = (row_codes[:, None] == col_codes[None, :]).astype(jnp.bfloat16)
    masked = (
        integrals.reshape(row_tiles, TILE, col_tiles, TILE) * allowed[:, None, :, None]
    ).reshape(row_count, col_count)
    occ_bit = lax.axis_size("occ").bit_length() - 2
    vir_bit = lax.axis_size("vir").bit_length() - 2
    row_local = jnp.remainder(row_mirror, amplitudes.shape[0])
    col_local = jnp.remainder(col_mirror, col_count)
    ladder = jnp.dot(
        amplitudes,
        lax.all_gather(masked, "occ", axis=0, tiled=True),
        preferred_element_type=jnp.float32,
    )
    partner = from_partner(ladder, "occ", occ_bit)
    rows_anti = ladder - jnp.take(partner, row_local, axis=0)
    across = from_partner(rows_anti, "vir", vir_bit)
    residual = rows_anti - jnp.take(across, col_local, axis=1)
    return residual / (occ_gap[:, None] + vir_energy[None, :])


def solution(mesh):
    placed = (P("occ", None), P("occ", "vir"), P(), P(), P("occ"), P("vir"), P("occ"), P("vir"))
    return jax.shard_map(
        local, mesh=mesh, in_specs=placed, out_specs=P("occ", "vir"), check_vma=False
    )
```

profile of v0, /device:TPU:32, one launch (start us, length us, event | category | flops | bytes accessed | tf_op | source)
XLA Modules:
  0.0 313.8 jit_solution(18139982531006995793)
XLA Ops:
  6.5 0.7 multiply_add_fusion
  7.2 0.1 fusion.3
  7.3 0.1 compare_convert_fusion
  7.4 0.2 mul.27
  7.6 1.9 bitcast_multiply_fusion
  9.5 0.0 all-gather.2.cloned.1.call-update
  9.5 0.0 copy-start.2
  9.5 118.8 %all-gather.2.cloned.1.call-done = bf16[8192,512]{1,0:T(8,128)(2,1)} async-done(((bf16[512,512]{1,0:T(8,128)(2,1)}), bf16[8192,512]{1,0:T(8,128)(2,1)}) %all-gather.2.cloned.1.call-update) | async-done | bytes 8388624 | tf_op jit(solution)/shard_map/all_gather | solution.py:33
  128.4 14.4 %convolution_bitcast_fusion = f32[1024,512]{0,1:T(8,128)S(1)} fusion(bf16[8192,512]{1,0:T(8,128)(2,1)} %all-gather.2.cloned.1.call-done, bf16[1024,8192]{1,0:T(8,128)(2,1)} %param.8), kind=kOutput, calls=%fused_computation.5 | convolution fusion | flops 8589934592 | bytes 27262976 | tf_op jit(solution)/shard_map/dot_general | solution.py:31
  142.8 0.0 copy-start.1
  142.8 2.6 collective-permute-start
  145.5 90.2 %collective-permute-done = f32[1024,512]{0,1:T(8,128)} collective-permute-done((f32[1024,512]{0,1:T(8,128)S(1)}, f32[1024,512]{0,1:T(8,128)}, u32[]{:S(2)}, u32[]{:S(2)}) %collective-permute-start) | collective-permute-done | bytes 2097184 | tf_op jit(solution)/shard_map/ppermute | solution.py:11
  235.6 1.9 copy.9
  237.6 4.9 %gather_fusion = f32[1024,512]{1,0:T(8,128)} fusion(f32[1024,512]{1,0:T(8,128)S(1)} %copy.9, s32[1024]{0:T(1024)S(1)} %broadcast_clamp_fusion), kind=kCustom, calls=%fused_computation | custom fusion | bytes 4198400 | tf_op jit(solution)/shard_map/jit(_take)/gather | solution.py:37
  242.5 1.9 copy.10
  244.4 0.0 copy-start.5
  244.4 2.0 select_subtract_fusion
  246.4 7.9 %collective-permute-start.1 = (f32[1024,512]{0,1:T(8,128)S(1)}, f32[1024,512]{0,1:T(8,128)S(1)}, u32[]{:S(2)}, u32[]{:S(2)}) collective-permute-start(f32[1024,512]{0,1:T(8,128)S(1)} %select_subtract_fusion), channel_id=1, source_target_pairs={{0,128},{16,144},{32,160},{48,176},{64,192},{80,208},{96,224},{112... | collective-permute-start | bytes 6291464 | tf_op jit(solution)/shard_map/ppermute | solution.py:11
  254.4 0.0 copy-start.3
  254.4 0.0 copy-start.4
  254.4 45.3 %collective-permute-done.1 = f32[1024,512]{0,1:T(8,128)S(1)} collective-permute-done((f32[1024,512]{0,1:T(8,128)S(1)}, f32[1024,512]{0,1:T(8,128)S(1)}, u32[]{:S(2)}, u32[]{:S(2)}) %collective-permute-start.1) | collective-permute-done | bytes 2097184 | tf_op jit(solution)/shard_map/ppermute | solution.py:11
  299.8 2.7 gather_fusion.1
  302.5 2.7 fusion
  305.1 1.8 copy.11
  (12 shorter events, 0.1 us)
Async XLA Ops:
  6.5 121.8 %all-gather.2.cloned.1.call-start = ((), (), s32[]{:S(2)}) async-start(), calls=%async_computation | async-start | bytes 8912896 | tf_op jit(solution)/shard_map/all_gather | solution.py:33
  9.5 135.9 %copy-start.2 = (s32[1024]{0:T(1024)S(1)}, s32[1024]{0:T(1024)}, u32[]{:S(2)}) copy-start(s32[1024]{0:T(1024)} %param.12) | copy-start | bytes 12292
  142.8 2.6 copy-start.1
  142.8 92.8 %collective-permute-start = (f32[1024,512]{0,1:T(8,128)S(1)}, f32[1024,512]{0,1:T(8,128)}, u32[]{:S(2)}, u32[]{:S(2)}) collective-permute-start(f32[1024,512]{0,1:T(8,128)S(1)} %convolution_bitcast_fusion), channel_id=1, source_target_pairs={{0,8},{1,9},{2,10},{3,11},{4,12},{5,13},{6,14},{7,15},{8,0},{9,1},... | collective-permute-start | bytes 6291464 | tf_op jit(solution)/shard_map/ppermute | solution.py:11
  244.4 10.0 %copy-start.5 = (s32[512]{0:T(512)S(1)}, s32[512]{0:T(512)}, u32[]{:S(2)}) copy-start(s32[512]{0:T(512)} %param.13) | copy-start | bytes 6148
  246.4 8.0 %copy-start = (f32[1024,512]{0,1:T(8,128)}, f32[1024,512]{0,1:T(8,128)S(1)}, u32[]{:S(2)}) copy-start(f32[1024,512]{0,1:T(8,128)S(1)} %select_subtract_fusion) | copy-start | bytes 6291460
  246.4 53.3 %collective-permute-start.1 = (f32[1024,512]{0,1:T(8,128)S(1)}, f32[1024,512]{0,1:T(8,128)S(1)}, u32[]{:S(2)}, u32[]{:S(2)}) collective-permute-start(f32[1024,512]{0,1:T(8,128)S(1)} %select_subtract_fusion), channel_id=1, source_target_pairs={{0,128},{16,144},{32,160},{48,176},{64,192},{80,208},{96,224},{112... | collective-permute-start | bytes 6291464 | tf_op jit(solution)/shard_map/ppermute | solution.py:11
  254.4 48.0 %copy-start.3 = (f32[1024]{0:T(1024)S(1)}, f32[1024]{0:T(1024)}, u32[]{:S(2)}) copy-start(f32[1024]{0:T(1024)} %param.14) | copy-start | bytes 12292
  254.4 48.0 %copy-start.4 = (f32[512]{0:T(512)S(1)}, f32[512]{0:T(512)}, u32[]{:S(2)}) copy-start(f32[512]{0:T(512)} %param.15) | copy-start | bytes 6148
Sparse Core Ops, SparseCore 0:
  9.8 118.5 all-gather.1
where the time goes:
time: 314 us
  waiting for transfers between devices  254 us (81%)
  matrix products  14.4 us (5%)
  local copies, waits for them, and re-layouts  13.6 us (4%)
  between operations  13.5 us (4%)
  starting transfers between devices  10.5 us (3%)
  other arithmetic  7.39 us (2%)
    ppermute x2, waiting for transfers between devices, from_partner(): lax.ppermute(x, axis, [(i, i ^ 1 << apart) for i in range(lax.axis_size(a...  136 us
    all_gather x1, waiting for transfers between devices, local(): lax.all_gather(masked, 'occ', axis=0, tiled=True)  119 us
    dot_general x1, matrix products, local(): jnp.dot(amplitudes, lax.all_gather(masked, 'occ', axis=0, tiled=True), pr...  14.4 us
    ppermute x2, starting transfers between devices, from_partner(): lax.ppermute(x, axis, [(i, i ^ 1 << apart) for i in range(lax.axis_size(a...  10.5 us
    gather x2, local copies, waits for them, and re-layouts, local(): rows_anti = ladder - jnp.take(partner, row_local, axis=0)  6.84 us
  transfers between devices with their start and end apart: 3, of which 3 were waited for; matrix products, arithmetic and copies ran while one was open for 0% of the time, Pallas kernels for 0%

commit v1 on v0

v1 whole, which is shorter than its diff:
```python
import functools
import jax
import jax.numpy as jnp
from jax import lax
from jax.sharding import PartitionSpec as P
from jax.experimental import pallas as pl
from jax.experimental.pallas import tpu as pltpu

TILE = 128
SPINS = 2
MESH = pl.DeviceIdType.MESH
CHUNK = 128
LEVELS = 32767.0
TINY = 1e-30
VMEM = pl.BlockSpec(memory_space=pltpu.VMEM)


def permuted(one_hot, x):
    hi = x.astype(jnp.bfloat16)
    lo = (x - hi.astype(jnp.float32)).astype(jnp.bfloat16)
    dot = functools.partial(jnp.dot, preferred_element_type=jnp.float32)
    return dot(one_hot, hi) + dot(one_hot, lo)


def permuted_cols(x, one_hot, transposed):
    hi = x.astype(jnp.bfloat16)
    lo = (x - hi.astype(jnp.float32)).astype(jnp.bfloat16)
    dims = (((1,), (1 if transposed else 0,)), ((), ()))
    dot = functools.partial(lax.dot_general, dimension_numbers=dims, preferred_element_type=jnp.float32)
    return dot(hi, one_hot) + dot(lo, one_hot)


def coded(x, top):
    return jnp.round(x * (LEVELS / top)).astype(jnp.int32).astype(jnp.int16)


def decoded(code, top):
    return code.astype(jnp.int32).astype(jnp.float32) * (top / LEVELS)


def exchange_kernel(
    ladder, row_here, row_there, col_there, out,
    own, sent_first, out_x1, in_x1, out_z, in_z, out_x2, in_x2, tops_out, tops_in, diff, to_rows, from_rows, cols,
    sends, recvs, top_sends, top_recvs,
):
    vir, occ = lax.axis_index("vir"), lax.axis_index("occ")
    virs, occs = lax.axis_size("vir"), lax.axis_size("occ")
    x_peer = (lax.rem(vir + virs // 2, virs), occ)
    z_peer = (vir, lax.rem(occ + occs // 2, occs))
    rows, width = ladder.shape
    half = width // 2
    chunks = rows // CHUNK
    lower = vir < virs // 2
    sign = jnp.where(lower, 1.0, -1.0).astype(jnp.float32)
    kept = pl.multiple_of(jnp.where(lower, 0, half), half)
    given = pl.multiple_of(half - kept, half)

    barrier = pltpu.get_barrier_semaphore()
    for peer in (x_peer, z_peer):
        pl.semaphore_signal(barrier, inc=1, device_id=peer, device_id_type=MESH)

    cols[...] = (
        lax.broadcasted_iota(jnp.int32, (width, width), 0)
        == jnp.where(lower, lax.broadcasted_iota(jnp.int32, (1, width), 1), col_there[...])
    ).astype(jnp.float32).astype(jnp.bfloat16)

    def make_to(c, _):
        at = pl.ds(pl.multiple_of(c * CHUNK, CHUNK), CHUNK)
        to_rows[at, :] = (
            lax.broadcasted_iota(jnp.int32, (CHUNK, rows), 0) + c * CHUNK == row_there[...]
        ).astype(jnp.float32).astype(jnp.bfloat16)
        return 0

    def make_from(c, _):
        at = pl.ds(pl.multiple_of(c * CHUNK, CHUNK), CHUNK)
        from_rows[at, :] = (
            lax.broadcasted_iota(jnp.int32, (CHUNK, rows), 1) == row_here[at, :][:, :1]
        ).astype(jnp.float32).astype(jnp.bfloat16)
        return 0

    lax.fori_loop(0, chunks, make_to, 0)

    def order_cols(c, _):
        at = pl.ds(pl.multiple_of(c * CHUNK, CHUNK), CHUNK)
        own[at, :] = permuted_cols(ladder[at, :], cols[...], True)
        return 0

    lax.fori_loop(0, chunks, order_cols, 0)

    def order_rows(c, _):
        at = pl.ds(pl.multiple_of(c * CHUNK, CHUNK), CHUNK)
        moved = permuted(to_rows[at, :], own[...])
        sent_first[at, :] = moved
        top = jnp.maximum(jnp.max(jnp.abs(moved), axis=0, keepdims=True), TINY)
        diff_top = top
        tops_out[0, pl.ds(c, 1), :] = diff_top[:, :half]
        tops_out[1, pl.ds(c, 1), :] = diff_top[:, half:]
        return 0

    lax.fori_loop(0, chunks, order_rows, 0)
    pl.semaphore_wait(barrier, 2)

    def tops(slot, source, peer):
        return pltpu.make_async_remote_copy(
            source, tops_in.at[slot], top_sends.at[slot], top_recvs.at[slot], device_id=peer, device_id_type=MESH
        )

    def piece(phase, c, source, target, peer):
        at = pl.ds(pl.multiple_of(c * CHUNK, CHUNK), CHUNK)
        return pltpu.make_async_remote_copy(
            source.at[at], target.at[at], sends.at[phase, c], recvs.at[phase, c], device_id=peer, device_id_type=MESH
        )

    keep_slot = jnp.where(lower, 0, 1)
    tops_out[2, :, :] = tops_out[1 - keep_slot, :, :]
    first_tops = tops(0, tops_out.at[2], x_peer)
    first_tops.start()

    def send_first(c, _):
        at = pl.ds(pl.multiple_of(c * CHUNK, CHUNK), CHUNK)
        out_x1[at, :] = coded(sent_first[at, pl.ds(given, half)], tops_out[2, pl.ds(c, 1), :])
        piece(0, c, out_x1, in_x1, x_peer).start()
        return 0

    lax.fori_loop(0, chunks, send_first, 0)
    lax.fori_loop(0, chunks, make_from, 0)

    first_tops.wait()
    tops_out[3, :, :] = tops_out[keep_slot, :, :] + tops_in[0, :, :]
    second_tops = tops(1, tops_out.at[3], z_peer)
    second_tops.start()

    def send_second(c, _):
        at = pl.ds(pl.multiple_of(c * CHUNK, CHUNK), CHUNK)
        piece(0, c, out_x1, in_x1, x_peer).wait()
        came = decoded(in_x1[at, :], tops_in[0, pl.ds(c, 1), :])
        diff[at, :] = came
        out_z[at, :] = coded(sign * (sent_first[at, pl.ds(kept, half)] - came), tops_out[3, pl.ds(c, 1), :])
        piece(1, c, out_z, in_z, z_peer).start()
        return 0

    lax.fori_loop(0, chunks, send_second, 0)
    second_tops.wait()

    def back(c, _):
        at = pl.ds(pl.multiple_of(c * CHUNK, CHUNK), CHUNK)
        mine = sign * (own[at, pl.ds(kept, half)] - permuted(from_rows[at, :], diff[...]))
        own[at, pl.ds(kept, half)] = mine
        tops_out[4, pl.ds(c, 1), :] = jnp.max(jnp.abs(mine), axis=0, keepdims=True) + tops_in[1, pl.ds(c, 1), :]
        return 0

    lax.fori_loop(0, chunks, back, 0)
    third_tops = tops(2, tops_out.at[4], x_peer)
    third_tops.start()

    def send_third(c, _):
        at = pl.ds(pl.multiple_of(c * CHUNK, CHUNK), CHUNK)
        piece(1, c, out_z, in_z, z_peer).wait()
        done = own[at, pl.ds(kept, half)] - decoded(in_z[at, :], tops_in[1, pl.ds(c, 1), :])
        own[at, pl.ds(kept, half)] = done
        out_x2[at, :] = coded(done, tops_out[4, pl.ds(c, 1), :])
        piece(2, c, out_x2, in_x2, x_peer).start()
        return 0

    lax.fori_loop(0, chunks, send_third, 0)
    third_tops.wait()

    def finish(c, _):
        at = pl.ds(pl.multiple_of(c * CHUNK, CHUNK), CHUNK)
        piece(2, c, out_x2, in_x2, x_peer).wait()
        own[at, pl.ds(given, half)] = decoded(in_x2[at, :], tops_in[2, pl.ds(c, 1), :])
        out[at, :] = sign * permuted_cols(own[at, :], cols[...], False)
        return 0

    lax.fori_loop(0, chunks, finish, 0)


def exchanged(ladder, row_local, col_local):
    rows, width = ladder.shape
    half = width // 2
    chunks = rows // CHUNK
    f32, i16, bf16 = jnp.float32, jnp.int16, jnp.bfloat16
    return pl.pallas_call(
        exchange_kernel,
        out_shape=jax.ShapeDtypeStruct((rows, width), f32),
        in_specs=[VMEM] * 4,
        out_specs=VMEM,
        scratch_shapes=[
            pltpu.VMEM((rows, width), f32),
            pltpu.VMEM((rows, width), f32),
        ]
        + [pltpu.VMEM((rows, half), i16)] * 6
        + [
            pltpu.VMEM((5, chunks, half), f32),
            pltpu.VMEM((3, chunks, half), f32),
            pltpu.VMEM((rows, half), f32),
            pltpu.VMEM((rows, rows), bf16),
            pltpu.VMEM((rows, rows), bf16),
            pltpu.VMEM((width, width), bf16),
            pltpu.SemaphoreType.DMA((3, chunks)),
            pltpu.SemaphoreType.DMA((3, chunks)),
            pltpu.SemaphoreType.DMA((3,)),
            pltpu.SemaphoreType.DMA((3,)),
        ],
        compiler_params=pltpu.CompilerParams(collective_id=1, has_side_effects=True, vmem_limit_bytes=48 << 20),
        name="exchange",
    )(ladder, jnp.broadcast_to(row_local[:, None], (rows, TILE)), row_local[None, :], col_local[None, :])


def local(amplitudes, integrals, tile_irrep, tile_spin, row_mirror, col_mirror, occ_gap, vir_energy):
    row_count, col_count = integrals.shape
    row_tiles = row_count // TILE
    col_tiles = col_count // TILE
    code = tile_irrep * SPINS + tile_spin
    row_codes = lax.dynamic_slice_in_dim(code, lax.axis_index("occ") * row_tiles, row_tiles)
    col_codes = lax.dynamic_slice_in_dim(code, lax.axis_index("vir") * col_tiles, col_tiles)
    allowed = row_codes[:, None] == col_codes[None, :]
    masked = jnp.where(
        allowed[:, None, :, None], integrals.reshape(row_tiles, TILE, col_tiles, TILE), 0
    ).reshape(row_count, col_count)
    row_local = jnp.remainder(row_mirror, amplitudes.shape[0])
    col_local = jnp.remainder(col_mirror, col_count)
    ladder = jnp.dot(
        amplitudes, lax.all_gather(masked, "occ", axis=0, tiled=True), preferred_element_type=jnp.float32
    )
    residual = exchanged(ladder, row_local, col_local)
    return residual / (occ_gap[:, None] + vir_energy[None, :])


def solution(mesh):
    placed = (P("occ", None), P("occ", "vir"), P(), P(), P("occ"), P("vir"), P("occ"), P("vir"))
    return jax.shard_map(
        local, mesh=mesh, in_specs=placed, out_specs=P("occ", "vir"), check_vma=False
    )
```

time: 314 us -> 197 us (0.63)
  waiting for transfers between devices: 254 us -> 119 us
  Pallas kernels: 0 us -> 43.4 us
  local copies, waits for them, and re-layouts: 13.6 us -> 0.5 us
  starting transfers between devices: 10.5 us -> 0.01 us
    ppermute x2 -> x0, waiting for transfers between devices: 136 us -> none  [from_partner(): lax.ppermute(x, axis, [(i, i ^ 1 << apart) for i in range(lax.axis_size(a...]
    pallas_call x0 -> x1, Pallas kernels: none -> 43.4 us  [exchanged(): pl.pallas_call(exchange_kernel, out_shape=jax.ShapeDtypeStruct((rows, wid...]
    ppermute x2 -> x0, starting transfers between devices: 10.5 us -> none  [from_partner(): lax.ppermute(x, axis, [(i, i ^ 1 << apart) for i in range(lax.axis_size(a...]
    gather x3 -> x0, local copies, waits for them, and re-layouts: 9.52 us -> none  [the longest x2 6.84 us: local(): rows_anti = ladder - jnp.take(partner, row_local, axis=0)]
  transfers between devices with their start and end apart: 3 -> 1, of which waited for: 3 -> 1; matrix products, arithmetic and copies ran while one was open for 0% -> 0% of each run, Pallas kernels for 0% -> 0%
where the time goes in v1:
time: 197 us; the launch traced here: 195 us
  waiting for transfers between devices  119 us (60%)
  Pallas kernels  43.4 us (22%)
  matrix products  14.3 us (7%)
  between operations  13.5 us (7%)
  other arithmetic  4.44 us (2%)
    all_gather x1, waiting for transfers between devices, local(): lax.all_gather(masked, 'occ', axis=0, tiled=True)  119 us
    pallas_call x1, Pallas kernels, exchanged(): pl.pallas_call(exchange_kernel, out_shape=jax.ShapeDtypeStruct((rows, wid...  43.4 us
    dot_general x1, matrix products, local(): jnp.dot(amplitudes, lax.all_gather(masked, 'occ', axis=0, tiled=True), pr...  14.3 us
  transfers between devices with their start and end apart: 1, of which 1 were waited for; matrix products, arithmetic and copies ran while one was open for 0% of the time, Pallas kernels for 0%

profile of v1, /device:TPU:32, one launch (start us, length us, event | category | flops | bytes accessed | tf_op | source)
XLA Modules:
  0.0 194.8 jit_solution(17196380096853139504)
XLA Ops:
  6.5 0.0 copy-start.3
  6.5 0.0 copy-start.1
  6.5 0.0 all-gather.2.cloned.1.call-start
  6.5 0.7 multiply_add_fusion
  7.2 0.1 fusion.2
  7.3 0.1 broadcast_compare_fusion
  7.4 0.2 broadcast_in_dim.31
  7.6 2.0 %bitcast_select_fusion = bf16[512,512]{1,0:T(8,128)(2,1)} fusion(bf16[512,512]{1,0:T(8,128)(2,1)} %param.9, pred[64,8,4,128]{3,2,1,0:T(4,128)(4,1)S(1)} %bitcast.12), kind=kLoop, calls=%fused_computation.2 | loop fusion | flops 262144 | bytes 1310720 | tf_op jit(solution)/shard_map/jit(_where)/select_n | solution.py:218
  9.6 0.0 all-gather.2.cloned.1.call-update
  9.6 0.0 copy-done.3
  9.6 0.0 copy-done.1
  9.7 118.7 %all-gather.2.cloned.1.call-done = bf16[8192,512]{1,0:T(8,128)(2,1)} async-done(((bf16[512,512]{1,0:T(8,128)(2,1)}), bf16[8192,512]{1,0:T(8,128)(2,1)}) %all-gather.2.cloned.1.call-update) | async-done | bytes 8388624 | tf_op jit(solution)/shard_map/all_gather | solution.py:224
  128.4 14.3 %convolution_bitcast_fusion.ladder = f32[1024,512]{1,0:T(8,128)S(1)} fusion(bf16[1024,8192]{1,0:T(8,128)(2,1)} %param.8, bf16[8192,512]{1,0:T(8,128)(2,1)} %all-gather.2.cloned.1.call-done), kind=kOutput, calls=%fused_computation.1 | convolution fusion | flops 8589934592 | bytes 27262976 | tf_op jit(solution)/shard_map/dot_general | solution.py:223
  142.7 0.2 broadcast_in_dim.34.row_here
  142.9 0.0 copy-start
  142.9 0.0 copy-start.2
  142.9 43.4 %exchange.1 = f32[1024,512]{1,0:T(8,128)S(1)} custom-call(f32[1024,512]{1,0:T(8,128)S(1)} %convolution_bitcast_fusion.ladder, s32[1024,128]{1,0:T(8,128)S(1)} %broadcast_in_dim.34.row_here, s32[1,1024]{1,0:T(1,128)S(1)} %bitcast.10, s32[1,512]{1,0:T(1,128)S(1)} %bitcast.11), custom_call_target="tpu_custom_call" | custom-call | tf_op jit(solution)/shard_map/exchange/pallas_call | solution.py:183
  186.3 0.0 copy-done
  186.3 0.0 copy-done.2
  186.3 1.7 add_divide_fusion
  (2 shorter events, 0.0 us)
Async XLA Ops:
  6.5 3.1 %copy-start.3 = (s32[512]{0:T(512)S(1)}, s32[512]{0:T(512)}, u32[]{:S(2)}) copy-start(s32[512]{0:T(512)} %param.13) | copy-start | bytes 6148
  6.5 3.1 %copy-start.1 = (s32[1024]{0:T(1024)S(1)}, s32[1024]{0:T(1024)}, u32[]{:S(2)}) copy-start(s32[1024]{0:T(1024)} %param.12) | copy-start | bytes 12292
  6.5 121.8 %all-gather.2.cloned.1.call-start = ((), (), s32[]{:S(2)}) async-start(), calls=%async_computation | async-start | bytes 8912896 | tf_op jit(solution)/shard_map/all_gather | solution.py:224
  142.9 43.4 %copy-start = (f32[1024]{0:T(1024)S(1)}, f32[1024]{0:T(1024)}, u32[]{:S(2)}) copy-start(f32[1024]{0:T(1024)} %param.14) | copy-start | bytes 12292
  142.9 43.4 %copy-start.2 = (f32[512]{0:T(512)S(1)}, f32[512]{0:T(512)}, u32[]{:S(2)}) copy-start(f32[512]{0:T(512)} %param.15) | copy-start | bytes 6148
Sparse Core Ops, SparseCore 0:
  9.8 118.5 all-gather.1

commit v2 on v1

--- a/solution.py
+++ b/solution.py
@@ -207,21 +207,271 @@
     )(ladder, jnp.broadcast_to(row_local[:, None], (rows, TILE)), row_local[None, :], col_local[None, :])
 
 
-def local(amplitudes, integrals, tile_irrep, tile_spin, row_mirror, col_mirror, occ_gap, vir_energy):
+SLOTS = 40
+TERMS = 18
+SLICES = 8
+FINE = TILE // SLICES
+SHARED = 16
+ROW_STEP = 256
+
+
+def ladder_kernel(
+    pack_from, term_slot, term_tile, blocks, amplitudes, ladder,
+    spread, tiles, amps, factor,
+    amp_sems, spread_sends, spread_recvs, z_sends, z_recvs, y_sends, y_recvs, core_sends, core_recvs,
+):
+    vir, occ = lax.axis_index("vir"), lax.axis_index("occ")
+    core, y, z = lax.rem(vir, 2), lax.rem(occ, 4), occ // 4
+    pair = vir - core
+    me = 2 * y + core
+    rows = ladder.shape[0]
+    half = SLOTS // 2
+
+    def beside(step):
+        to = lax.rem(me + step, SLICES)
+        return to, (pair + lax.rem(to, 2), z * 4 + to // 2)
+
+    def along_z(step):
+        return (vir, lax.rem(z + step, 4) * 4 + y)
+
+    def along_y(step):
+        return (vir, z * 4 + lax.rem(y + step, 4))
+
+    mate = (pair + 1 - core, occ)
+
+    barrier = pltpu.get_barrier_semaphore()
+    for step in range(1, SLICES):
+        pl.semaphore_signal(barrier, inc=1, device_id=beside(step)[1], device_id_type=MESH)
+    for step in range(1, 4):
+        pl.semaphore_signal(barrier, inc=1, device_id=along_z(step), device_id_type=MESH)
+
+    parts = rows // ROW_STEP
+
+    columns = amps.shape[0]
+
+    def load(c):
+        lanes = pl.ds(pl.multiple_of(c * TILE, TILE), TILE)
+        return pltpu.make_async_copy(amplitudes.at[:, lanes], amps.at[c], amp_sems.at[c])
+
+    def load_start(c, _):
+        load(c).start()
+        return 0
+
+    def load_wait(c, _):
+        load(c).wait()
+        return 0
+
+    lax.fori_loop(0, columns, load_start, 0)
+    tiles[4 * SLOTS] = jnp.zeros((TILE, TILE), jnp.bfloat16)
+    pl.semaphore_wait(barrier, SLICES - 1 + 3)
+
+    lane_tiles = blocks.shape[3] // TILE
+
+    def spread_ends(to, lane):
+        return (
+            blocks.at[:, to, :, pl.ds(lane * TILE, TILE)],
+            spread.at[pl.ds((lane_tiles * core + lane) * SHARED + 4 * y, 4)],
+        )
+
+    def spread_copy(step, lane):
+        to, peer = beside(step)
+        return pltpu.make_async_remote_copy(
+            *spread_ends(to, lane), spread_sends.at[step, lane], spread_recvs.at[step, lane],
+            device_id=peer, device_id_type=MESH,
+        )
+
+    copies = [spread_copy(step, lane) for step in range(1, SLICES) for lane in range(lane_tiles)]
+    copies += [pltpu.make_async_copy(*spread_ends(me, lane), spread_recvs.at[0, lane]) for lane in range(lane_tiles)]
+    for copy in copies:
+        copy.start()
+    for copy in copies:
+        copy.wait()
+
+    mine = pl.ds(pl.multiple_of(me * FINE, FINE), FINE)
+
+    def pack(s, _):
+        tiles[z * SLOTS + s, mine, :] = spread[pack_from[s]]
+        return 0
+
+    lax.fori_loop(0, SLOTS, pack, 0)
+
+    def shard(origin_z, origin_y, first, count):
+        at = pl.ds(lax.rem(origin_z, 4) * SLOTS + first, count)
+        band = pl.ds(pl.multiple_of((2 * lax.rem(origin_y, 4) + core) * FINE, FINE), FINE)
+        return tiles.at[at, band, :]
+
+    def remote(ref, send, recv, peer):
+        return pltpu.make_async_remote_copy(ref, ref, send, recv, device_id=peer, device_id_type=MESH)
+
+    z_copies = {
+        step: remote(shard(z, y, 0, SLOTS), z_sends.at[step], z_recvs.at[step], along_z(step)) for step in (1, 3, 2)
+    }
+    started = []
+
+    def begin(copy):
+        copy.start()
+        started.append(copy)
+
+    def landed(ref, recv):
+        remote(ref, z_sends.at[0], recv, mate).wait_recv()
+
+    def to_mate(d, e):
+        begin(remote(shard(z + 4 - d, y + 4 - e, 0, SLOTS), core_sends.at[d, e], core_recvs.at[d, e], mate))
+
+    def to_sides(d):
+        ref = shard(z + 4 - d, y, 0, SLOTS)
+        begin(remote(ref, y_sends.at[d, 0], y_recvs.at[d, 0], along_y(1)))
+        begin(remote(ref, y_sends.at[d, 1], y_recvs.at[d, 1], along_y(3)))
+        to_mate(d, 0)
+
+    def from_sides(d):
+        landed(shard(z + 4 - d, y + 3, 0, SLOTS), y_recvs.at[d, 0])
+        begin(remote(shard(z + 4 - d, y + 3, 0, half), y_sends.at[d, 2], y_recvs.at[d, 2], along_y(1)))
+        landed(shard(z + 4 - d, y + 1, 0, SLOTS), y_recvs.at[d, 1])
+        begin(remote(shard(z + 4 - d, y + 1, half, SLOTS - half), y_sends.at[d, 3], y_recvs.at[d, 3], along_y(3)))
+        to_mate(d, 1)
+        to_mate(d, 3)
+
+    def from_across(d):
+        landed(shard(z + 4 - d, y + 2, 0, half), y_recvs.at[d, 2])
+        landed(shard(z + 4 - d, y + 2, half, SLOTS - half), y_recvs.at[d, 3])
+        to_mate(d, 2)
+
+    def from_z(d):
+        landed(shard(z + 4 - d, y, 0, SLOTS), z_recvs.at[d])
+        to_sides(d)
+
+    for step in (1, 3, 2):
+        begin(z_copies[step])
+    to_sides(0)
+    from_z(1)
+    from_z(3)
+    from_sides(0)
+    from_z(2)
+    from_sides(1)
+    from_sides(3)
+    from_across(0)
+    from_sides(2)
+    from_across(1)
+    from_across(3)
+    from_across(2)
+    lax.fori_loop(0, columns, load_wait, 0)
+    for copy in started:
+        copy.wait_send()
+    for d in range(4):
+        for e in range(4):
+            at = pl.ds(lax.rem(z + 4 - d, 4) * SLOTS, SLOTS)
+            band = pl.ds(pl.multiple_of((2 * lax.rem(y + 4 - e, 4) + 1 - core) * FINE, FINE), FINE)
+            landed(tiles.at[at, band, :], core_recvs.at[d, e])
+
+    for t in range(ladder.shape[1] // TILE):
+        lanes = pl.ds(t * TILE, TILE)
+        for k in range(TERMS):
+            factor[pl.ds(k * TILE, TILE), :] = tiles[term_slot[t * TERMS + k]]
+
+        def product(c, _):
+            at = pl.ds(pl.multiple_of(c * ROW_STEP, ROW_STEP), ROW_STEP)
+            left = jnp.concatenate(
+                [amps[term_tile[t * TERMS + k], at, :] for k in range(TERMS)], axis=1
+            )
+            ladder[at, lanes] = jnp.dot(left, factor[...], preferred_element_type=jnp.float32)
+            return 0
+
+        lax.fori_loop(0, parts, product, 0)
+
+
+def tile_lists(code):
+    tiles = code.shape[0]
+    number = jnp.arange(tiles, dtype=jnp.int32)
+    zone, pair = number // SHARED, number // 8
+    equal = code[:, None] == code[None, :]
+    earlier = equal & (number[:, None] < number[None, :])
+    rank = jnp.sum(earlier, axis=0, dtype=jnp.int32)
+    zone_rank = jnp.sum(earlier & (zone[:, None] == zone[None, :]), axis=0, dtype=jnp.int32)
+    members = jnp.sum(equal.reshape(4, SHARED, tiles), axis=1, dtype=jnp.int32)
+    before = (pair[:, None] == pair[None, :]) & (number[:, None] < number[None, :])
+    start = jnp.sum(jnp.where(before[None], members[:, :, None], 0), axis=1, dtype=jnp.int32)
+    slot = jnp.repeat(start, SHARED, axis=0) + zone_rank[:, None]
+    fits = (jnp.max(jnp.sum(members, axis=0)) <= TERMS) & (
+        jnp.max(jnp.sum(members.reshape(4, tiles // 8, 8), axis=2)) <= SLOTS
+    )
+    return equal, rank, slot, fits
+
+
+def own_lists(equal, rank, slot):
+    vir, occ = lax.axis_index("vir"), lax.axis_index("occ")
+    where = (occ // 4 * SHARED, vir // 2 * 8)
+    kept = lax.dynamic_slice(equal, where, (SHARED, 8))
+    at = jnp.where(kept, lax.dynamic_slice(slot, where, (SHARED, 8)), -1)
+    hit = at[None] == jnp.arange(SLOTS, dtype=jnp.int32)[:, None, None]
+    down, across = lax.broadcasted_iota(jnp.int32, (SHARED, 8), 0), lax.broadcasted_iota(jnp.int32, (SHARED, 8), 1)
+    pack_from = jnp.sum(jnp.where(hit, (across * SHARED + down)[None], 0), axis=(1, 2))
+    tiles = equal.shape[0]
+    number = jnp.arange(tiles, dtype=jnp.int32)
+    cols = (0, vir * 4)
+    kept = lax.dynamic_slice(equal, cols, (tiles, 4))
+    at = lax.dynamic_slice(slot, cols, (tiles, 4)) + (number // SHARED * SLOTS)[:, None]
+    hit = kept[:, :, None] & (rank[:, None, None] == jnp.arange(TERMS, dtype=jnp.int32)[None, None, :])
+    term_tile = jnp.sum(jnp.where(hit, number[:, None, None], 0), axis=0)
+    term_slot = 4 * SLOTS + jnp.sum(jnp.where(hit, at[:, :, None] - 4 * SLOTS, 0), axis=0)
+    return pack_from, term_slot.reshape(-1), term_tile.reshape(-1)
+
+
+def kept_ladder(amplitudes, integrals, lists):
+    rows, width = amplitudes.shape[0], integrals.shape[1]
+    bf16 = jnp.bfloat16
+    smem = pl.BlockSpec(memory_space=pltpu.SMEM)
+    dma = pltpu.SemaphoreType.DMA
+    return pl.pallas_call(
+        ladder_kernel,
+        out_shape=jax.ShapeDtypeStruct((rows, width), jnp.float32),
+        in_specs=[smem] * 3 + [VMEM, pl.BlockSpec(memory_space=pl.ANY)],
+        out_specs=VMEM,
+        scratch_shapes=[
+            pltpu.VMEM((2 * width // TILE * SHARED, FINE, TILE), bf16),
+            pltpu.VMEM((4 * SLOTS + 1, TILE, TILE), bf16),
+            pltpu.VMEM((amplitudes.shape[1] // TILE, rows, TILE), bf16),
+            pltpu.VMEM((TERMS * TILE, TILE), bf16),
+            dma((amplitudes.shape[1] // TILE,)),
+            dma((SLICES, width // TILE)),
+            dma((SLICES, width // TILE)),
+            dma((4,)),
+            dma((4,)),
+            dma((4, 4)),
+            dma((4, 4)),
+            dma((4, 4)),
+            dma((4, 4)),
+        ],
+        compiler_params=pltpu.CompilerParams(collective_id=2, has_side_effects=True, vmem_limit_bytes=48 << 20),
+        name="kept_ladder",
+    )(*lists, integrals.reshape(integrals.shape[0] // TILE, SLICES, FINE, width), amplitudes)
+
+
+def full_ladder(amplitudes, integrals, code):
     row_count, col_count = integrals.shape
     row_tiles = row_count // TILE
     col_tiles = col_count // TILE
-    code = tile_irrep * SPINS + tile_spin
     row_codes = lax.dynamic_slice_in_dim(code, lax.axis_index("occ") * row_tiles, row_tiles)
     col_codes = lax.dynamic_slice_in_dim(code, lax.axis_index("vir") * col_tiles, col_tiles)
     allowed = row_codes[:, None] == col_codes[None, :]
     masked = jnp.where(
         allowed[:, None, :, None], integrals.reshape(row_tiles, TILE, col_tiles, TILE), 0
     ).reshape(row_count, col_count)
+    return jnp.dot(
+        amplitudes, lax.all_gather(masked, "occ", axis=0, tiled=True), preferred_element_type=jnp.float32
+    )
+
+
+def local(amplitudes, integrals, tile_irrep, tile_spin, row_mirror, col_mirror, occ_gap, vir_energy):
+    code = tile_irrep * SPINS + tile_spin
     row_local = jnp.remainder(row_mirror, amplitudes.shape[0])
-    col_local = jnp.remainder(col_mirror, col_count)
-    ladder = jnp.dot(
-        amplitudes, lax.all_gather(masked, "occ", axis=0, tiled=True), preferred_element_type=jnp.float32
+    col_local = jnp.remainder(col_mirror, integrals.shape[1])
+    equal, rank, slot, fits = tile_lists(code)
+    lists = own_lists(equal, rank, slot)
+    ladder = lax.cond(
+        fits,
+        lambda: kept_ladder(amplitudes, integrals, lists),
+        lambda: full_ladder(amplitudes, integrals, code),
     )
     residual = exchanged(ladder, row_local, col_local)
     return residual / (occ_gap[:, None] + vir_energy[None, :])

time: 197 us -> 123 us (0.62); the launches traced: 195 us -> 123 us
  waiting for transfers between devices: 119 us -> 0 us
  Pallas kernels: 43.4 us -> 102 us
  matrix products: 14.3 us -> 0 us
    all_gather x1 -> x0, waiting for transfers between devices: 119 us -> none  [local(): lax.all_gather(masked, 'occ', axis=0, tiled=True)]
    pallas_call x0 -> x1, Pallas kernels: none -> 57.5 us  [kept_ladder(): pl.pallas_call(ladder_kernel, out_shape=jax.ShapeDtypeStruct((rows, width...]
    dot_general x1 -> x0, matrix products: 14.3 us -> none  [local(): jnp.dot(amplitudes, lax.all_gather(masked, 'occ', axis=0, tiled=True), pr...]
  transfers between devices with their start and end apart: 1 -> 0, of which waited for: 1 -> 0; matrix products, arithmetic and copies ran while one was open for 0% -> 0% of each run, Pallas kernels for 0% -> 0%
where the time goes in v2:
time: 123 us
  Pallas kernels  102 us (83%)
  between operations  14.8 us (12%)
  other arithmetic  5.29 us (4%)
    pallas_call x1, Pallas kernels, kept_ladder(): pl.pallas_call(ladder_kernel, out_shape=jax.ShapeDtypeStruct((rows, width...  57.5 us
    pallas_call x1, Pallas kernels, exchanged(): pl.pallas_call(exchange_kernel, out_shape=jax.ShapeDtypeStruct((rows, wid...  44.4 us

profile of v2, /device:TPU:32, one launch (start us, length us, event | category | flops | bytes accessed | tf_op | source)
XLA Modules:
  0.0 123.1 jit_solution(15710938135766460122)
XLA Ops:
  6.5 0.7 and_select_fusion
  7.3 0.1 constant_dynamic-slice_fusion
  7.4 0.1 copy.28
  7.5 0.1 convert_reduce_fusion.3
  7.6 0.1 eq.104
  7.7 0.1 convert_reduce_fusion
  7.8 0.1 fusion.2
  7.9 0.1 select_reduce_fusion.3
  8.1 0.1 reshape.197
  8.2 0.1 reduce_sum.83
  8.4 0.6 reduce_max.19
  9.7 0.6 reduce_max.18
  11.0 58.9 %conditional.1 = (f32[1024,512]{1,0:T(8,128)S(1)}) conditional(s32[]{:T(128)} %convert_element_type.15, (s32[64]{0:T(128)S(1)}, bf16[512,512]{1,0:T(8,128)(2,1)}, bf16[1024,8192]{1,0:T(8,128)(2,1)}) %tuple.11, (bf16[512,512]{1,0:T(8,128)(2,1)}, pred[64,64]{1,0:T(8,128)(4,1)S(1)}, pred[64,4,18]{0,1,2:T(4,128)(4,1)S(1)}, ...), branch_computations={%region_11.12_spmd, %region_12.13_spmd} | conditional | flops 8590196736 | bytes 59769160 | solution.py:471
  11.0 0.1 dynamic-slice_select_fusion
  11.1 0.1 select_reduce_fusion.pack_from
  11.3 0.7 select_reduce_fusion.2
  12.0 0.1 copy.31
  12.1 0.1 add.121.term_slot
  12.2 0.1 copy.27
  12.3 0.1 reshape.200.term_tile
  12.4 57.5 %kept_ladder.1 = f32[1024,512]{1,0:T(8,128)S(1)} custom-call(s32[40]{0:T(128)S(1)} %select_reduce_fusion.pack_from, s32[72]{0:T(128)S(1)} %add.121.term_slot, s32[72]{0:T(128)S(1)} %reshape.200.term_tile, bf16[4,8,16,512]{3,2,1,0:T(8,128)(2,1)} %bitcast.15, bf16[1024,8192]{1,0:T(8,128)(2,1)} %get-tuple-element.31.amplitudes), custom_call_target="tpu_custom_call" | custom-call | tf_op jit(solution)/shard_map/cond/branch_1_fun/kept_ladder/pallas_call | solution.py:425
  69.9 0.2 broadcast_in_dim.124.row_here
  70.2 44.4 %exchange.1 = f32[1024,512]{1,0:T(8,128)S(1)} custom-call(f32[1024,512]{1,0:T(8,128)S(1)} %get-tuple-element.243.ladder, s32[1024,128]{1,0:T(8,128)S(1)} %broadcast_in_dim.124.row_here, s32[1,1024]{1,0:T(1,128)S(1)} %bitcast.13, s32[1,512]{1,0:T(1,128)S(1)} %bitcast.14), custom_call_target="tpu_custom_call" | custom-call | tf_op jit(solution)/shard_map/exchange/pallas_call | solution.py:183
  114.6 1.7 %add_divide_fusion = f32[1024,512]{1,0:T(8,128)} fusion(f32[1024,512]{1,0:T(8,128)S(1)} %exchange.1, f32[512]{0:T(512)S(1)} %copy-done.2, f32[1024]{0:T(1024)S(1)} %copy-done), kind=kLoop, calls=%fused_computation.13 | loop fusion | flops 1048576 | bytes 4200448 | tf_op jit(solution)/shard_map/div | solution.py:477
  (25 shorter events, 0.4 us)
Async XLA Ops:
  11.0 58.9 %copy-start.1 = (s32[1024]{0:T(1024)S(1)}, s32[1024]{0:T(1024)}, u32[]{:S(2)}) copy-start(s32[1024]{0:T(1024)} %param.14) | copy-start | bytes 12292
  11.0 59.1 %copy-start.3 = (s32[512]{0:T(512)S(1)}, s32[512]{0:T(512)}, u32[]{:S(2)}) copy-start(s32[512]{0:T(512)} %param.15) | copy-start | bytes 6148
  70.1 44.4 %copy-start = (f32[1024]{0:T(1024)S(1)}, f32[1024]{0:T(1024)}, u32[]{:S(2)}) copy-start(f32[1024]{0:T(1024)} %param.16) | copy-start | bytes 12292
  70.1 44.4 %copy-start.2 = (f32[512]{0:T(512)S(1)}, f32[512]{0:T(512)}, u32[]{:S(2)}) copy-start(f32[512]{0:T(512)} %param.17) | copy-start | bytes 6148

commit v3 on v0

v3 whole, which is shorter than its diff:
```python
import functools
import jax
import jax.numpy as jnp
from jax import lax
from jax.sharding import PartitionSpec as P
from jax.experimental import pallas as pl
from jax.experimental.pallas import tpu as pltpu

TILE = 128
SPINS = 2
MESH = pl.DeviceIdType.MESH
CHUNK = 128
BLOCK = 512
LEVELS = 32767.0
TINY = 1e-30
SLICES = 8
FINE = TILE // SLICES
SHARED = 16
ZONES = 4
FORMS = ((40, 18),)
VMEM = pl.BlockSpec(memory_space=pltpu.VMEM)
F32, BF16 = jnp.float32, jnp.bfloat16
dot = functools.partial(jnp.dot, preferred_element_type=F32)


def span(c, size):
    return pl.ds(pl.multiple_of(c * size, size), size)


def loop(count, body):
    def step(c, _):
        body(c)
        return 0

    lax.fori_loop(0, count, step, 0)


def upright(line):
    size = line.shape[1]
    square = lax.broadcasted_iota(jnp.int32, (size, size), 0) == lax.broadcasted_iota(jnp.int32, (size, size), 1)
    return jnp.sum(jnp.where(square, line, 0), axis=1, keepdims=True, dtype=jnp.int32)


def halves(x):
    hi = x.astype(BF16)
    return hi, (x - hi.astype(F32)).astype(BF16)


def coded(x, top):
    return jnp.round(x * (LEVELS / top)).astype(jnp.int32).astype(jnp.int16)


def decoded(code, top):
    return code.astype(jnp.int32).astype(F32) * (top / LEVELS)


def place():
    vir, occ = lax.axis_index("vir"), lax.axis_index("occ")
    return vir, occ, lax.axis_size("vir"), lax.axis_size("occ")


def mirror_peers():
    vir, occ, virs, occs = place()
    return (lax.rem(vir + virs // 2, virs), occ), (vir, lax.rem(occ + occs // 2, occs))


def one_hots(row_there, col_there, to_rows, from_rows, cols):
    vir, _, virs, _ = place()
    rows, width = to_rows.shape[0], cols.shape[0]
    target = jnp.where(
        vir < virs // 2, lax.broadcasted_iota(jnp.int32, (1, width), 1), col_there[...] & (width - 1)
    )
    cols[...] = (lax.broadcasted_iota(jnp.int32, (width, width), 0) == target).astype(F32).astype(BF16)

    def make(c):
        at = span(c, CHUNK)
        down = lax.broadcasted_iota(jnp.int32, (CHUNK, rows), 0) + c * CHUNK
        to_rows[at, :] = (down == row_there[...] & (rows - 1)).astype(F32).astype(BF16)
        across = lax.broadcasted_iota(jnp.int32, (CHUNK, rows), 1)
        from_rows[at, :] = (across == upright(row_there[:, at] & (rows - 1))).astype(F32).astype(BF16)

    loop(rows // CHUNK, make)


def exchange_steps(
    ladder, out, own, there, split, out_x1, in_x1, out_z, in_z, out_x2, in_x2, tops_out, tops_in,
    to_rows, from_rows, cols, sends, recvs, top_sends, top_recvs,
):
    vir, _, virs, _ = place()
    x_peer, z_peer = mirror_peers()
    rows, width = ladder.shape
    half = width // 2
    chunks, blocks = rows // CHUNK, rows // BLOCK
    per_block = BLOCK // CHUNK
    lower = vir < virs // 2
    sign = jnp.where(lower, 1.0, -1.0).astype(F32)
    kept = pl.multiple_of(jnp.where(lower, 0, half), half)
    given = pl.multiple_of(half - kept, half)

    def tops(slot, peer):
        return pltpu.make_async_remote_copy(
            tops_out.at[slot], tops_in.at[slot], top_sends.at[slot], top_recvs.at[slot],
            device_id=peer, device_id_type=MESH,
        )

    def piece(phase, c, source, target, peer):
        at = span(c, CHUNK)
        return pltpu.make_async_remote_copy(
            source.at[at], target.at[at], sends.at[phase, c], recvs.at[phase, c], device_id=peer, device_id_type=MESH
        )

    def first(c):
        return piece(0, c, out_x1, in_x1, x_peer)

    def second(c):
        return piece(1, c, out_z, in_z, z_peer)

    def third(c):
        return piece(2, c, out_x2, in_x2, x_peer)

    def joined(x):
        return x[:, :half] + x[:, half:]

    def store_split(at, x):
        split[at, :half], split[at, half:] = halves(x)

    def in_order(columns, keep):
        wanted = cols[pl.ds(columns, half), :]

        def order(b):
            at = span(b, BLOCK)
            pair = jnp.concatenate(halves(ladder[at, :]), axis=0)
            x = lax.dot_general(pair, wanted, (((1,), (1,)), ((), ())), preferred_element_type=F32)
            x = x[:BLOCK] + x[BLOCK:]
            if keep:
                own[at, :] = x
            store_split(at, x)

        loop(blocks, order)

    in_order(given, False)

    def code_first(b):
        moved = joined(dot(to_rows[span(b, BLOCK), :], split[...]))
        for s in range(per_block):
            c = b * per_block + s
            part = moved[s * CHUNK : (s + 1) * CHUNK]
            top = jnp.maximum(jnp.max(jnp.abs(part), axis=0, keepdims=True), TINY)
            tops_out[0, pl.ds(c, 1), :] = top
            out_x1[span(c, CHUNK), :] = coded(part, top)

    loop(blocks, code_first)
    tops(0, x_peer).start()
    loop(chunks, lambda c: first(c).start())

    in_order(kept, True)

    def move_kept(b):
        moved = joined(dot(to_rows[span(b, BLOCK), :], split[...]))
        there[span(b, BLOCK), :] = moved
        for s in range(per_block):
            part = moved[s * CHUNK : (s + 1) * CHUNK]
            tops_out[1, pl.ds(b * per_block + s, 1), :] = jnp.max(jnp.abs(part), axis=0, keepdims=True)

    loop(blocks, move_kept)
    tops(0, x_peer).wait()
    tops_out[1, :, :] = tops_out[1, :, :] + tops_in[0, :, :]
    tops(1, z_peer).start()

    def send_second(c):
        at, top = span(c, CHUNK), pl.ds(c, 1)
        first(c).wait()
        came = decoded(in_x1[at, :], tops_in[0, top, :])
        store_split(at, came)
        out_z[at, :] = coded(sign * (there[at, :] - came), tops_out[1, top, :])
        second(c).start()

    loop(chunks, send_second)
    tops(1, z_peer).wait()

    def back(b):
        at = span(b, BLOCK)
        mine = sign * (own[at, :] - joined(dot(from_rows[at, :], split[...])))
        own[at, :] = mine
        for s in range(per_block):
            top = pl.ds(b * per_block + s, 1)
            part = mine[s * CHUNK : (s + 1) * CHUNK]
            tops_out[2, top, :] = jnp.max(jnp.abs(part), axis=0, keepdims=True) + tops_in[1, top, :]

    loop(blocks, back)
    tops(2, x_peer).start()

    def send_third(c):
        at, top = span(c, CHUNK), pl.ds(c, 1)
        second(c).wait()
        done = own[at, :] - decoded(in_z[at, :], tops_in[1, top, :])
        own[at, :] = done
        out_x2[at, :] = coded(done, tops_out[2, top, :])
        third(c).start()

    loop(chunks, send_third)
    tops(2, x_peer).wait()

    def finish(c):
        at = span(c, CHUNK)
        third(c).wait()
        came = decoded(in_x2[at, :], tops_in[2, pl.ds(c, 1), :])
        ours = jnp.concatenate(halves(own[at, :]), axis=0)
        theirs = jnp.concatenate(halves(came), axis=0)
        x = dot(ours, cols[pl.ds(kept, half), :]) + dot(theirs, cols[pl.ds(given, half), :])
        out[at, :] = sign * (x[:CHUNK] + x[CHUNK:])

    loop(chunks, finish)


def exchange_kernel(ladder, row_there, col_there, out, *scratch):
    barrier = pltpu.get_barrier_semaphore()
    for peer in mirror_peers():
        pl.semaphore_signal(barrier, inc=1, device_id=peer, device_id_type=MESH)
    to_rows, from_rows, cols = scratch[-7:-4]
    one_hots(row_there, col_there, to_rows, from_rows, cols)
    pl.semaphore_wait(barrier, 2)
    exchange_steps(ladder, out, *scratch)


def exchange_scratch(rows, width):
    half, chunks = width // 2, rows // CHUNK
    dma = pltpu.SemaphoreType.DMA
    return (
        [pltpu.VMEM((rows, half), F32)] * 2
        + [pltpu.VMEM((rows, width), BF16)]
        + [pltpu.VMEM((rows, half), jnp.int16)] * 6
        + [pltpu.VMEM((3, chunks, half), F32)] * 2
        + [pltpu.VMEM((rows, rows), BF16)] * 2
        + [pltpu.VMEM((width, width), BF16)]
        + [dma((3, chunks))] * 2
        + [dma((3,))] * 2
    )


def mirror_tables(row_mirror, col_mirror):
    return row_mirror[None, :], col_mirror[None, :]


def exchanged(ladder, row_mirror, col_mirror):
    return pl.pallas_call(
        exchange_kernel,
        out_shape=jax.ShapeDtypeStruct(ladder.shape, F32),
        in_specs=[VMEM] * 3,
        out_specs=VMEM,
        scratch_shapes=exchange_scratch(*ladder.shape),
        compiler_params=pltpu.CompilerParams(collective_id=1, has_side_effects=True, vmem_limit_bytes=48 << 20),
        name="exchange",
    )(ladder, *mirror_tables(row_mirror, col_mirror))


def ladder_steps(
    slots, terms, lists, blocks, amplitudes, ladder, meanwhile,
    spread, tiles, amps, factor,
    amp_sems, spread_sends, spread_recvs, z_sends, z_recvs, y_sends, y_recvs, core_sends, core_recvs,
):
    vir, occ, _, _ = place()
    core, y, z = lax.rem(vir, 2), lax.rem(occ, 4), occ // 4
    pair = vir - core
    me = 2 * y + core
    rows, width = ladder.shape
    lane_tiles = width // TILE
    columns = amps.shape[0]
    half = slots // 2

    def beside(step):
        to = lax.rem(me + step, SLICES)
        return to, (pair + lax.rem(to, 2), z * 4 + to // 2)

    def along_z(step):
        return (vir, lax.rem(z + step, 4) * 4 + y)

    def along_y(step):
        return (vir, z * 4 + lax.rem(y + step, 4))

    mate = (pair + 1 - core, occ)
    barrier = pltpu.get_barrier_semaphore()
    peers = [beside(step)[1] for step in range(1, SLICES)] + [along_z(step) for step in (1, 2, 3)] + [mirror_peers()[0]]
    for peer in peers:
        pl.semaphore_signal(barrier, inc=1, device_id=peer, device_id_type=MESH)

    def load(c):
        return pltpu.make_async_copy(amplitudes.at[:, span(c, TILE)], amps.at[c], amp_sems.at[c])

    loop(columns, lambda c: load(c).start())
    tiles[ZONES * slots] = jnp.zeros((TILE, TILE), BF16)
    pl.semaphore_wait(barrier, len(peers))

    def ends(to, lane):
        return (
            blocks.at[:, to, :, pl.ds(lane * TILE, TILE)],
            spread.at[pl.ds((lane_tiles * core + lane) * SHARED + 4 * y, 4)],
        )

    def spread_copy(step, lane):
        to, peer = beside(step)
        return pltpu.make_async_remote_copy(
            *ends(to, lane), spread_sends.at[step, lane], spread_recvs.at[step, lane],
            device_id=peer, device_id_type=MESH,
        )

    copies = [spread_copy(step, lane) for step in range(1, SLICES) for lane in range(lane_tiles)]
    copies += [pltpu.make_async_copy(*ends(me, lane), spread_recvs.at[0, lane]) for lane in range(lane_tiles)]
    for copy in copies:
        copy.start()
    meanwhile()
    for copy in copies:
        copy.wait()

    mine = span(me, FINE)

    def pack(s):
        tiles[z * slots + s, mine, :] = spread[lists[0, s]]

    loop(slots, pack)

    def shard(d, e, part, other=False):
        at = pl.ds(lax.rem(z + 4 - d, 4) * slots + part * half, half)
        owner = 2 * lax.rem(y + 4 - e, 4) + (1 - core if other else core)
        return tiles.at[at, span(owner, FINE), :]

    started = []

    def send(ref, send_sem, recv_sem, peer):
        copy = pltpu.make_async_remote_copy(ref, ref, send_sem, recv_sem, device_id=peer, device_id_type=MESH)
        copy.start()
        started.append(copy)

    def landed(ref, recv_sem):
        pltpu.make_async_remote_copy(
            ref, ref, z_sends.at[0, 0], recv_sem, device_id=mate, device_id_type=MESH
        ).wait_recv()

    def to_mate(d, e, part):
        send(shard(d, e, part), core_sends.at[d, e, part], core_recvs.at[d, e, part], mate)

    def z_out(part):
        for step in (1, 3):
            send(shard(0, 0, part), z_sends.at[step, part], z_recvs.at[step, part], along_z(step))

    def y_out(d, part):
        for step in (1, 3):
            send(shard(d, 0, part), y_sends.at[d, step, part], y_recvs.at[d, step, part], along_y(step))
        to_mate(d, 0, part)

    def z_in(part):
        near, far = (1, 3) if part == 0 else (3, 1)
        landed(shard(near, 0, part), z_recvs.at[near, part])
        send(shard(near, 0, part), z_sends.at[2, part], z_recvs.at[2, part], along_z(near))
        y_out(near, part)
        landed(shard(far, 0, part), z_recvs.at[far, part])
        y_out(far, part)

    def z_across(part):
        landed(shard(2, 0, part), z_recvs.at[2, part])
        y_out(2, part)

    def y_in(d, part):
        near, far = (1, 3) if part == 0 else (3, 1)
        landed(shard(d, near, part), y_recvs.at[d, near, part])
        send(shard(d, near, part), y_sends.at[d, 2, part], y_recvs.at[d, 2, part], along_y(near))
        to_mate(d, near, part)
        landed(shard(d, far, part), y_recvs.at[d, far, part])
        to_mate(d, far, part)

    def y_across(d, part):
        landed(shard(d, 2, part), y_recvs.at[d, 2, part])
        to_mate(d, 2, part)

    for part in (0, 1):
        z_out(part)
        y_out(0, part)
    y_in(0, 0)
    y_in(0, 1)
    z_in(0)
    y_across(0, 0)
    z_in(1)
    y_across(0, 1)
    y_in(1, 0)
    y_in(3, 0)
    z_across(0)
    y_in(3, 1)
    y_in(1, 1)
    z_across(1)
    for d, part in ((1, 0), (3, 0), (3, 1), (1, 1)):
        y_across(d, part)
    y_in(2, 0)
    y_in(2, 1)
    y_across(2, 0)
    y_across(2, 1)
    loop(columns, lambda c: load(c).wait())
    for copy in started:
        copy.wait_send()
    for d in range(4):
        for e in range(4):
            for part in (0, 1):
                landed(shard(d, e, part, True), core_recvs.at[d, e, part])

    for t in range(lane_tiles):
        for k in range(terms):
            factor[pl.ds(k * TILE, TILE), :] = tiles[lists[1 + t, k]]

        def product(b):
            at = span(b, BLOCK // 2)
            left = jnp.concatenate([amps[lists[1 + lane_tiles + t, k], at, :] for k in range(terms)], axis=1)
            ladder[at, pl.ds(t * TILE, TILE)] = dot(left, factor[...])

        loop(rows // (BLOCK // 2), product)


def ladder_scratch(rows, summed, width, slots, terms):
    dma = pltpu.SemaphoreType.DMA
    return [
        pltpu.VMEM((2 * width // TILE * SHARED, FINE, TILE), BF16),
        pltpu.VMEM((ZONES * slots + 1, TILE, TILE), BF16),
        pltpu.VMEM((summed // TILE, rows, TILE), BF16),
        pltpu.VMEM((terms * TILE, TILE), BF16),
        dma((summed // TILE,)),
        dma((SLICES, width // TILE)),
        dma((SLICES, width // TILE)),
        dma((4, 2)),
        dma((4, 2)),
        dma((4, 4, 2)),
        dma((4, 4, 2)),
        dma((4, 4, 2)),
        dma((4, 4, 2)),
    ]


def fused_kernel(slots, terms, count, lists, row_there, col_there, blocks, amplitudes, out, ladder, *scratch):
    swap = scratch[:count]
    meanwhile = functools.partial(one_hots, row_there, col_there, *swap[-7:-4])
    ladder_steps(slots, terms, lists, blocks, amplitudes, ladder, meanwhile, *scratch[count:])
    exchange_steps(ladder, out, *swap)


def packed(form, lists, amplitudes, integrals, row_mirror, col_mirror):
    slots, terms = FORMS[form]
    (rows, summed), width = amplitudes.shape, integrals.shape[1]
    swap = exchange_scratch(rows, width)
    return pl.pallas_call(
        functools.partial(fused_kernel, slots, terms, len(swap)),
        out_shape=jax.ShapeDtypeStruct((rows, width), F32),
        in_specs=[pl.BlockSpec(memory_space=pltpu.SMEM)] + [VMEM] * 3 + [pl.BlockSpec(memory_space=pl.ANY)],
        out_specs=VMEM,
        scratch_shapes=[pltpu.VMEM((rows, width), F32)] + swap + ladder_scratch(rows, summed, width, slots, terms),
        compiler_params=pltpu.CompilerParams(
            collective_id=2 + form, has_side_effects=True, vmem_limit_bytes=56 << 20
        ),
        name="packed",
    )(
        lists,
        *mirror_tables(row_mirror, col_mirror),
        integrals.reshape(integrals.shape[0] // TILE, SLICES, FINE, width),
        amplitudes,
    )


def lists_kernel(irrep, spin, lists):
    vir, occ, _, _ = place()
    across = irrep[...] * SPINS + spin[...]
    down = upright(across)
    tiles = down.shape[0]
    number = lax.broadcasted_iota(jnp.int32, (tiles, tiles), 0)
    other = lax.broadcasted_iota(jnp.int32, (tiles, tiles), 1)
    equal = down == across
    one = jnp.where(equal, 1, 0)
    prior = jnp.where(other < number, one, 0)
    total = functools.partial(jnp.sum, keepdims=True, dtype=jnp.int32)
    rank = total(prior, axis=1)
    zone_rank = total(jnp.where(other // SHARED == number // SHARED, prior, 0), axis=1)
    before = (number < other) & (number // 8 == other // 8)
    slot = zone_rank + jnp.zeros((tiles, tiles), jnp.int32)
    widest = jnp.zeros((1, 1), jnp.int32)
    for zone in range(ZONES):
        members = total(jnp.where(other // SHARED == zone, one, 0), axis=1)
        start = total(jnp.where(before, members, 0), axis=0)
        slot += jnp.where(number // SHARED == zone, start, 0)
        group = total(jnp.where(number // 8 == other // 8, members, 0), axis=0)
        widest = jnp.maximum(widest, jnp.max(group, axis=1, keepdims=True))
    longest = jnp.max(total(one, axis=0), axis=1, keepdims=True)
    form = jnp.full((1, 1), len(FORMS), jnp.int32)
    stride = jnp.zeros((1, 1), jnp.int32)
    for f, (slots, terms) in reversed(list(enumerate(FORMS))):
        fits = (widest <= slots) & (longest <= terms)
        form = jnp.where(fits, f, form)
        stride = jnp.where(fits, slots, stride)

    entry = lax.broadcasted_iota(jnp.int32, (tiles, TILE), 1)
    tile = lax.broadcasted_iota(jnp.int32, (tiles, TILE), 0)

    def column(x, a):
        return total(jnp.where(other == a, x, 0), axis=1)

    pack = jnp.zeros((1, TILE), jnp.int32)
    here = tile // SHARED == occ // 4
    for a in range(8):
        hit = here & (column(one, vir // 2 * 8 + a) == 1) & (column(slot, vir // 2 * 8 + a) == entry)
        pack += total(jnp.where(hit, a * SHARED + tile % SHARED, 0), axis=0)
    lists[0:1, :] = pack
    for t in range(4):
        a = vir * 4 + t
        hit = (column(one, a) == 1) & (rank == entry)
        at = tile // SHARED * stride + column(slot, a) - ZONES * stride
        lists[1 + t : 2 + t, :] = ZONES * stride + total(jnp.where(hit, at, 0), axis=0)
        lists[5 + t : 6 + t, :] = total(jnp.where(hit, tile, 0), axis=0)
    lists[9:10, :] = form + jnp.zeros((1, TILE), jnp.int32)


def tile_lists(tile_irrep, tile_spin):
    return pl.pallas_call(
        lists_kernel,
        out_shape=jax.ShapeDtypeStruct((16, TILE), jnp.int32),
        in_specs=[VMEM] * 2,
        out_specs=VMEM,
        name="lists",
    )(tile_irrep[None, :], tile_spin[None, :])


def full_ladder(amplitudes, integrals, code):
    row_count, col_count = integrals.shape
    row_tiles = row_count // TILE
    col_tiles = col_count // TILE
    row_codes = lax.dynamic_slice_in_dim(code, lax.axis_index("occ") * row_tiles, row_tiles)
    col_codes = lax.dynamic_slice_in_dim(code, lax.axis_index("vir") * col_tiles, col_tiles)
    allowed = row_codes[:, None] == col_codes[None, :]
    masked = jnp.where(
        allowed[:, None, :, None], integrals.reshape(row_tiles, TILE, col_tiles, TILE), 0
    ).reshape(row_count, col_count)
    return jnp.dot(amplitudes, lax.all_gather(masked, "occ", axis=0, tiled=True), preferred_element_type=F32)


def local(amplitudes, integrals, tile_irrep, tile_spin, row_mirror, col_mirror, occ_gap, vir_energy):
    lists = tile_lists(tile_irrep, tile_spin)

    def whole():
        ladder = full_ladder(amplitudes, integrals, tile_irrep * SPINS + tile_spin)
        return exchanged(ladder, row_mirror, col_mirror)

    forms = [
        functools.partial(packed, form, lists, amplitudes, integrals, row_mirror, col_mirror)
        for form in range(len(FORMS))
    ]
    residual = lax.switch(lists[9, 0], forms + [whole])
    return residual / (occ_gap[:, None] + vir_energy[None, :])


def solution(mesh):
    placed = (P("occ", None), P("occ", "vir"), P(), P(), P("occ"), P("vir"), P("occ"), P("vir"))
    return jax.shard_map(local, mesh=mesh, in_specs=placed, out_specs=P("occ", "vir"), check_vma=False)
```

time: 314 us -> 111 us (0.35)
  waiting for transfers between devices: 254 us -> 0 us
  Pallas kernels: 0 us -> 93.1 us
  matrix products: 14.4 us -> 0 us
  local copies, waits for them, and re-layouts: 13.6 us -> 0.53 us
  starting transfers between devices: 10.5 us -> 0 us
  other arithmetic: 7.39 us -> 1.67 us
    ppermute x2 -> x0, waiting for transfers between devices: 136 us -> none  [from_partner(): lax.ppermute(x, axis, [(i, i ^ 1 << apart) for i in range(lax.axis_size(a...]
    all_gather x1 -> x0, waiting for transfers between devices: 119 us -> none  [local(): lax.all_gather(masked, 'occ', axis=0, tiled=True)]
    pallas_call x0 -> x2, Pallas kernels: none -> 93.1 us  [the longest x1 91.6 us: packed(): pl.pallas_call(functools.partial(fused_kernel, slots, terms, len(swap)),...]
    dot_general x1 -> x0, matrix products: 14.4 us -> none  [local(): jnp.dot(amplitudes, lax.all_gather(masked, 'occ', axis=0, tiled=True), pr...]
    ppermute x2 -> x0, starting transfers between devices: 10.5 us -> none  [from_partner(): lax.ppermute(x, axis, [(i, i ^ 1 << apart) for i in range(lax.axis_size(a...]
    gather x3 -> x0, local copies, waits for them, and re-layouts: 9.52 us -> none  [the longest x2 6.84 us: local(): rows_anti = ladder - jnp.take(partner, row_local, axis=0)]
  transfers between devices with their start and end apart: 3 -> 0, of which waited for: 3 -> 0; matrix products, arithmetic and copies ran while one was open for 0% -> 0% of each run, Pallas kernels for 0% -> 0%
where the time goes in v3:
time: 111 us; the launch traced here: 110 us
  Pallas kernels  93.1 us (84%)
  between operations  14.1 us (13%)
  other arithmetic  1.67 us (2%)
    pallas_call x1, Pallas kernels, packed(): pl.pallas_call(functools.partial(fused_kernel, slots, terms, len(swap)),...  91.6 us

profile of v3, /device:TPU:32, one launch (start us, length us, event | category | flops | bytes accessed | tf_op | source)
XLA Modules:
  0.0 109.6 jit_solution(16329028700963076747)
XLA Ops:
  6.5 1.4 %lists.1 = s32[16,128]{1,0:T(8,128)S(1)} custom-call(s32[1,64]{1,0:T(1,128)} %bitcast.22, s32[1,64]{1,0:T(1,128)} %bitcast.23), custom_call_target="tpu_custom_call" | custom-call | tf_op jit(solution)/shard_map/lists/pallas_call | solution.py:516
  7.9 0.5 slice.4
  9.1 0.0 copy-start.2
  9.1 0.0 copy-start.3
  9.1 91.9 %conditional.1 = (f32[1024,512]{1,0:T(8,128)S(1)}) conditional(s32[]{:T(128)} %bitcast.8, (s32[1024]{0:T(1024)}, s32[512]{0:T(512)}, bf16[512,512]{1,0:T(8,128)(2,1)}, s32[16,128]{1,0:T(8,128)S(1)}, bf16[1024,8192]{1,0:T(8,128)(2,1)}) %tuple.11, (s32[64]{0:T(128)}, s32[64]{0:T(128)}, bf16[512,512]{1,0:T(8,128)(2,1)}, bf16[1024,8192]{1,0:T(8,128)(2,1)}, ...), branch_computations={%region_0.0_spmd, %region_1.2_spmd} | conditional | flops 8590196736 | bytes 55600256 | solution.py:549
  9.2 91.6 %packed.1 = f32[1024,512]{1,0:T(8,128)S(1)} custom-call(s32[16,128]{1,0:T(8,128)S(1)} %get-tuple-element.30.lists, s32[1,1024]{1,0:T(1,128)} %bitcast.18, s32[1,512]{1,0:T(1,128)} %bitcast.20, bf16[4,8,16,512]{3,2,1,0:T(8,128)(2,1)} %bitcast.16, bf16[1024,8192]{1,0:T(8,128)(2,1)} %get-tuple-element.34.amplitudes), custom_call_target="tpu_custom_call" | custom-call | tf_op jit(solution)/shard_map/cond/branch_0_fun/packed/pallas_call | solution.py:446
  101.0 0.0 copy-done.2
  101.0 0.0 copy-done.3
  101.1 1.7 %add_divide_fusion = f32[1024,512]{1,0:T(8,128)} fusion(f32[1024,512]{1,0:T(8,128)S(1)} %get-tuple-element.43, f32[512]{0:T(512)S(1)} %copy-done.3, f32[1024]{0:T(1024)S(1)} %copy-done.2), kind=kLoop, calls=%fused_computation.4 | loop fusion | flops 1048576 | bytes 4200448 | tf_op jit(solution)/shard_map/div | solution.py:550
Async XLA Ops:
  9.1 91.9 %copy-start.2 = (f32[1024]{0:T(1024)S(1)}, f32[1024]{0:T(1024)}, u32[]{:S(2)}) copy-start(f32[1024]{0:T(1024)} %param.16) | copy-start | bytes 12292
  9.1 91.9 %copy-start.3 = (f32[512]{0:T(512)S(1)}, f32[512]{0:T(512)}, u32[]{:S(2)}) copy-start(f32[512]{0:T(512)} %param.17) | copy-start | bytes 6148

commit v4 on v3

--- a/solution.py
+++ b/solution.py
@@ -17,7 +17,7 @@
 FINE = TILE // SLICES
 SHARED = 16
 ZONES = 4
-FORMS = ((40, 18),)
+FORMS = ((28, 14), (34, 16), (52, 22))
 VMEM = pl.BlockSpec(memory_space=pltpu.VMEM)
 F32, BF16 = jnp.float32, jnp.bfloat16
 dot = functools.partial(jnp.dot, preferred_element_type=F32)
@@ -405,12 +405,8 @@
         for k in range(terms):
             factor[pl.ds(k * TILE, TILE), :] = tiles[lists[1 + t, k]]
 
-        def product(b):
-            at = span(b, BLOCK // 2)
-            left = jnp.concatenate([amps[lists[1 + lane_tiles + t, k], at, :] for k in range(terms)], axis=1)
-            ladder[at, pl.ds(t * TILE, TILE)] = dot(left, factor[...])
-
-        loop(rows // (BLOCK // 2), product)
+        left = jnp.concatenate([amps[lists[1 + lane_tiles + t, k]] for k in range(terms)], axis=1)
+        ladder[:, pl.ds(t * TILE, TILE)] = dot(left, factor[...])
 
 
 def ladder_scratch(rows, summed, width, slots, terms):

time: 111 us -> 105 us (0.946); the launches traced: 110 us -> 105 us
  Pallas kernels: 93.1 us -> 87.8 us
    pallas_call x1, Pallas kernels: 91.6 us -> 86.4 us  [packed(): pl.pallas_call(functools.partial(fused_kernel, slots, terms, len(swap)),...]
where the time goes in v4:
time: 105 us
  Pallas kernels  87.8 us (84%)
  between operations  14.1 us (13%)
  other arithmetic  1.67 us (2%)
    pallas_call x1, Pallas kernels, packed(): pl.pallas_call(functools.partial(fused_kernel, slots, terms, len(swap)),...  86.4 us

profile of v4, /device:TPU:32, one launch (start us, length us, event | category | flops | bytes accessed | tf_op | source)
XLA Modules:
  0.0 104.8 jit_solution(2739468229644364360)
XLA Ops:
  6.5 1.4 %lists.1 = s32[16,128]{1,0:T(8,128)S(1)} custom-call(s32[1,64]{1,0:T(1,128)} %bitcast.34, s32[1,64]{1,0:T(1,128)} %bitcast.35), custom_call_target="tpu_custom_call" | custom-call | tf_op jit(solution)/shard_map/lists/pallas_call | solution.py:512
  8.0 0.5 slice.4
  9.1 0.0 copy-start.2
  9.1 0.0 copy-start.3
  9.1 87.1 %conditional.1 = (f32[1024,512]{1,0:T(8,128)S(1)}) conditional(s32[]{:T(128)} %bitcast.14, (s32[1024]{0:T(1024)}, s32[512]{0:T(512)}, bf16[512,512]{1,0:T(8,128)(2,1)}, s32[16,128]{1,0:T(8,128)S(1)}, bf16[1024,8192]{1,0:T(8,128)(2,1)}) %tuple.17, (s32[1024]{0:T(1024)}, s32[512]{0:T(512)}, bf16[512,512]{1,0:T(8,128)(2,1)}, ...), branch_computations={%region_0.0_spmd, %region_1.0_spmd, %region_2.0_spmd, %region_3.4_... | conditional | flops 8590196736 | bytes 55600256 | solution.py:545
  9.4 86.4 %packed.4 = f32[1024,512]{1,0:T(8,128)S(1)} custom-call(s32[16,128]{1,0:T(8,128)S(1)} %get-tuple-element.57.lists, s32[1,1024]{1,0:T(1,128)} %bitcast.27, s32[1,512]{1,0:T(1,128)} %bitcast.31, bf16[4,8,16,512]{3,2,1,0:T(8,128)(2,1)} %bitcast.23, bf16[1024,8192]{1,0:T(8,128)(2,1)} %get-tuple-element.61.amplitudes), custom_call_target="tpu_custom_call" | custom-call | tf_op jit(solution)/shard_map/cond/branch_1_fun/packed/pallas_call | solution.py:442
  96.3 0.0 copy-done.2
  96.3 0.0 copy-done.3
  96.3 1.7 %add_divide_fusion = f32[1024,512]{1,0:T(8,128)} fusion(f32[1024,512]{1,0:T(8,128)S(1)} %get-tuple-element.75, f32[512]{0:T(512)S(1)} %copy-done.3, f32[1024]{0:T(1024)S(1)} %copy-done.2), kind=kLoop, calls=%fused_computation.4 | loop fusion | flops 1048576 | bytes 4200448 | tf_op jit(solution)/shard_map/div | solution.py:546
Async XLA Ops:
  9.1 87.1 %copy-start.2 = (f32[1024]{0:T(1024)S(1)}, f32[1024]{0:T(1024)}, u32[]{:S(2)}) copy-start(f32[1024]{0:T(1024)} %param.18) | copy-start | bytes 12292
  9.1 87.1 %copy-start.3 = (f32[512]{0:T(512)S(1)}, f32[512]{0:T(512)}, u32[]{:S(2)}) copy-start(f32[512]{0:T(512)} %param.19) | copy-start | bytes 6148

commit v5 on v4

--- a/solution.py
+++ b/solution.py
@@ -17,7 +17,7 @@
 FINE = TILE // SLICES
 SHARED = 16
 ZONES = 4
-FORMS = ((28, 14), (34, 16), (52, 22))
+FORMS = ((28, 14), (32, 16), (38, 18), (56, 24))
 VMEM = pl.BlockSpec(memory_space=pltpu.VMEM)
 F32, BF16 = jnp.float32, jnp.bfloat16
 dot = functools.partial(jnp.dot, preferred_element_type=F32)
@@ -457,7 +457,7 @@
     )
 
 
-def lists_kernel(irrep, spin, lists):
+def lists_kernel(irrep, spin, lists, chosen):
     vir, occ, _, _ = place()
     across = irrep[...] * SPINS + spin[...]
     down = upright(across)
@@ -505,15 +505,15 @@
         at = tile // SHARED * stride + column(slot, a) - ZONES * stride
         lists[1 + t : 2 + t, :] = ZONES * stride + total(jnp.where(hit, at, 0), axis=0)
         lists[5 + t : 6 + t, :] = total(jnp.where(hit, tile, 0), axis=0)
-    lists[9:10, :] = form + jnp.zeros((1, TILE), jnp.int32)
+    chosen[0, 0] = jnp.max(form)
 
 
 def tile_lists(tile_irrep, tile_spin):
     return pl.pallas_call(
         lists_kernel,
-        out_shape=jax.ShapeDtypeStruct((16, TILE), jnp.int32),
+        out_shape=(jax.ShapeDtypeStruct((16, TILE), jnp.int32), jax.ShapeDtypeStruct((1, 1), jnp.int32)),
         in_specs=[VMEM] * 2,
-        out_specs=VMEM,
+        out_specs=(VMEM, pl.BlockSpec(memory_space=pltpu.SMEM)),
         name="lists",
     )(tile_irrep[None, :], tile_spin[None, :])
 
@@ -532,7 +532,7 @@
 
 
 def local(amplitudes, integrals, tile_irrep, tile_spin, row_mirror, col_mirror, occ_gap, vir_energy):
-    lists = tile_lists(tile_irrep, tile_spin)
+    lists, chosen = tile_lists(tile_irrep, tile_spin)
 
     def whole():
         ladder = full_ladder(amplitudes, integrals, tile_irrep * SPINS + tile_spin)
@@ -542,7 +542,7 @@
         functools.partial(packed, form, lists, amplitudes, integrals, row_mirror, col_mirror)
         for form in range(len(FORMS))
     ]
-    residual = lax.switch(lists[9, 0], forms + [whole])
+    residual = lax.switch(chosen[0, 0], forms + [whole])
     return residual / (occ_gap[:, None] + vir_energy[None, :])
 
 

time: 105 us -> 104 us (level)
  no operation moved by 1% of the time
where the time goes in v5:
time: 104 us; the launch traced here: 105 us
  Pallas kernels  88.1 us (85%)
  between operations  14.1 us (14%)
  other arithmetic  1.67 us (2%)
    pallas_call x1, Pallas kernels, packed(): pl.pallas_call(functools.partial(fused_kernel, slots, terms, len(swap)),...  86.4 us

profile of v5, /device:TPU:32, one launch (start us, length us, event | category | flops | bytes accessed | tf_op | source)
XLA Modules:
  0.0 104.6 jit_solution(8802480797577570657)
XLA Ops:
  6.5 1.7 %lists.1 = (s32[16,128]{1,0:T(8,128)S(1)}, s32[1,1]{1,0:T(1,128)}) custom-call(s32[1,64]{1,0:T(1,128)} %bitcast.40, s32[1,64]{1,0:T(1,128)} %bitcast.41), custom_call_target="tpu_custom_call" | custom-call | tf_op jit(solution)/shard_map/lists/pallas_call | solution.py:512
  8.9 0.0 copy-start.2
  8.9 0.0 copy-start.3
  8.9 87.2 %conditional.1 = (f32[1024,512]{1,0:T(8,128)S(1)}) conditional(s32[]{:T(128)} %bitcast.17, (s32[1024]{0:T(1024)}, s32[512]{0:T(512)}, bf16[512,512]{1,0:T(8,128)(2,1)}, s32[16,128]{1,0:T(8,128)S(1)}, bf16[1024,8192]{1,0:T(8,128)(2,1)}) %tuple.20, (s32[1024]{0:T(1024)}, s32[512]{0:T(512)}, bf16[512,512]{1,0:T(8,128)(2,1)}, ...), branch_computations={%region_0.0_spmd, %region_1.0_spmd, %region_2.0_spmd, %region_3.0_... | conditional | flops 8590196736 | bytes 55600256 | solution.py:545
  9.1 86.4 %packed.5 = f32[1024,512]{1,0:T(8,128)S(1)} custom-call(s32[16,128]{1,0:T(8,128)S(1)} %get-tuple-element.68.lists, s32[1,1024]{1,0:T(1,128)} %bitcast.31, s32[1,512]{1,0:T(1,128)} %bitcast.36, bf16[4,8,16,512]{3,2,1,0:T(8,128)(2,1)} %bitcast.26, bf16[1024,8192]{1,0:T(8,128)(2,1)} %get-tuple-element.72.amplitudes), custom_call_target="tpu_custom_call" | custom-call | tf_op jit(solution)/shard_map/cond/branch_1_fun/packed/pallas_call | solution.py:442
  96.1 0.0 copy-done.2
  96.1 0.0 copy-done.3
  96.1 1.7 %add_divide_fusion = f32[1024,512]{1,0:T(8,128)} fusion(f32[1024,512]{1,0:T(8,128)S(1)} %get-tuple-element.95, f32[512]{0:T(512)S(1)} %copy-done.3, f32[1024]{0:T(1024)S(1)} %copy-done.2), kind=kLoop, calls=%fused_computation.4 | loop fusion | flops 1048576 | bytes 4200448 | tf_op jit(solution)/shard_map/div | solution.py:546
Async XLA Ops:
  8.9 87.2 %copy-start.2 = (f32[1024]{0:T(1024)S(1)}, f32[1024]{0:T(1024)}, u32[]{:S(2)}) copy-start(f32[1024]{0:T(1024)} %param.19) | copy-start | bytes 12292
  8.9 87.2 %copy-start.3 = (f32[512]{0:T(512)S(1)}, f32[512]{0:T(512)}, u32[]{:S(2)}) copy-start(f32[512]{0:T(512)} %param.20) | copy-start | bytes 6148
